TPU v7x, 32 devices: a whole 2x2x4 slice. The times are simulated.
32 devices in a mesh: group: 2 (over y), box: 16 (over z, x, core).
Axes of the slice: x: 2, y: 2, z: 4, core: 2. Of those that a mesh axis runs over, the one named last changes fastest.
Arguments:
- dipoles: float32 [3, 8192], P(None, ('group', 'box')), may hold values from -6 to 6
- perm_field: float32 [3, 8192], P(None, ('group', 'box')), may hold values from -6 to 6
- positions: float32 [3, 8192], P(None, ('group', 'box')), may hold values from -1 to 1
- polarizability: float32 [8192], P(('group', 'box')), may hold values from 0.5 to 2.5
- occupancy: int32 [64], P(('group', 'box')), may hold values from 1 to 128
- far_boxes: int32 [64, 189], P(('group', 'box')), may hold values from 0 to 63, as said below
- far_class: int32 [64, 189], P(('group', 'box')), may hold values from 0 to 7
- far_count: int32 [64], P(('group', 'box')), may hold values from 94 to 189
- far_scale: float32 [64, 189], P(('group', 'box')), may hold values from 0.2 to 1
- translations: float32 [8, 165, 165], replicated, may hold values from -0.0015015624 to 0.0015015624
Outputs:
- new_dipoles: float32 [3, 8192], P(None, ('group', 'box'))
- residual: float32 [3, 8192], P(None, ('group', 'box'))
Inputs may be any that keep to these rules, and one draw needn't show every extreme that they name: Entry far_boxes[b, e] names a box of layer z' in group g' with |z' - z| <= 4 for box b's own layer z and group g, and |z' - z| >= 2 where g' = g; the first entry of every list is 4 layers away.
All inputs are finite; a program needn't handle non-finite values.
Results may differ from a plain program's by a relative error of at most 0.0003.
Values sent between devices are 32-bit elements; how exact they have to be, the bound alone decides.
A program may use at most 64 MiB of HBM per device.

v0:
```python
import jax
import jax.numpy as jnp
import numpy as np
from jax import lax
from jax.sharding import PartitionSpec as P

TILE = 128
ORDER = 8
NTERM = 165
FX = 2
FY = 1
REACH = 4
CLASSES = 8


HALF = 5.4
THOLE = 0.39
SOFT = 1.0
HIGH = lax.Precision.HIGHEST


def extended(block, sides, width):
    for axis, dim in sides:
        count = lax.axis_size(axis)
        forward = [(i, i + 1) for i in range(count - 1)]
        backward = [(target, source) for source, target in forward]
        low = lax.ppermute(
            lax.slice_in_dim(block, block.shape[dim] - width, None, axis=dim), axis, forward
        )
        high = lax.ppermute(lax.slice_in_dim(block, 0, width, axis=dim), axis, backward)
        block = jnp.concatenate([low, block, high], axis=dim)
    return block


def from_behind(x, axis, by):
    peers = lax.axis_size(axis)
    pairs = [(i, i + by) for i in range(peers) if 0 <= i + by < peers]
    return lax.ppermute(x, axis, pairs)


def term_table(order):
    listing = []
    for degree in range(order + 1):
        for first_idx in range(degree + 1):
            for second_idx in range(degree + 1 - first_idx):
                listing.append((first_idx, second_idx, degree - first_idx - second_idx))
    return np.array(listing, dtype=np.int32)


def chebyshev(coord, order):
    series = [jnp.ones_like(coord), coord]
    for number in range(2, order + 1):
        series.append(2.0 * coord * series[-1] - series[-2])
    return jnp.stack(series[: order + 1])


def monomials(positions):
    table = term_table(ORDER)
    cheb_x = chebyshev(positions[0], ORDER)
    cheb_y = chebyshev(positions[1], ORDER)
    cheb_z = chebyshev(positions[2], ORDER)
    return cheb_x[table[:, 0]] * cheb_y[table[:, 1]] * cheb_z[table[:, 2]]


def pair_field(target_rel, target_root, source_rel, source_root, source_dip, offset, keep_mask):
    deltas = [
        HALF
        * (
            target_rel[component][:, :, None]
            - source_rel[component][:, None, :]
            - 2.0 * offset[component]
        )
        for component in range(3)
    ]
    squared = deltas[0] * deltas[0] + deltas[1] * deltas[1] + deltas[2] * deltas[2] + SOFT
    inverse = lax.rsqrt(squared)
    cube_inv = inverse * inverse * inverse
    strength = (
        THOLE * squared * jnp.sqrt(squared) * target_root[:, :, None] * source_root[:, None, :]
    )
    damping = jnp.exp(-strength)
    lambda_three = -jnp.expm1(-strength)
    lambda_five = lambda_three - strength * damping
    projection = (
        deltas[0] * source_dip[0][:, None, :]
        + deltas[1] * source_dip[1][:, None, :]
        + deltas[2] * source_dip[2][:, None, :]
    )
    radial = keep_mask * 3.0 * lambda_five * cube_inv * inverse * inverse * projection
    direct = keep_mask * lambda_three * cube_inv
    return jnp.stack(
        [
            jnp.sum(deltas[component] * radial - direct * source_dip[component][:, None, :], axis=2)
            for component in range(3)
        ]
    )


def near_operator(dipole_src, geometry, target_rel, target_root):
    box_dev = FX * FY
    shaped = dipole_src.reshape(3, 1, FX, FY, TILE)
    layers = extended(shaped, (("box", 1),), 1)
    padded = jnp.pad(layers, ((0, 0), (0, 0), (1, 1), (1, 1), (0, 0)))
    total = jnp.zeros((3, box_dev, TILE), jnp.float32)
    for shift_z in (-1, 0, 1):
        for shift_x in (-1, 0, 1):
            for shift_y in (-1, 0, 1):
                window_dip = padded[
                    :, 1 + shift_z, 1 + shift_x : 1 + shift_x + FX, 1 + shift_y : 1 + shift_y + FY
                ].reshape(3, box_dev, TILE)
                window_geo = geometry[
                    :, 1 + shift_z, 1 + shift_x : 1 + shift_x + FX, 1 + shift_y : 1 + shift_y + FY
                ].reshape(4, box_dev, TILE)
                if shift_z == 0 and shift_x == 0 and (shift_y == 0):
                    keep_mask = 1.0 - jnp.eye(TILE, dtype=jnp.float32)
                else:
                    keep_mask = jnp.float32(1.0)
                total = total + pair_field(
                    target_rel,
                    target_root,
                    window_geo[:3],
                    window_geo[3],
                    window_dip,
                    (float(shift_x), float(shift_y), float(shift_z)),
                    keep_mask,
                )
    return total.reshape(3, -1)


def far_field(source, monomial, far_boxes, far_class, far_count, far_scale, translations):
    box_dev = far_boxes.shape[0]
    mono_b = monomial.reshape(NTERM, box_dev, TILE)
    dip_b = source.reshape(3, box_dev, TILE)
    multipole = jnp.einsum("tbs,cbs->bct", mono_b, dip_b, precision=HIGH).reshape(
        box_dev, 3 * NTERM
    )
    owners = lax.axis_size("box")
    layer = lax.axis_index("box")
    span = 2 * REACH + 1
    device = far_boxes // box_dev
    stride = device % owners - layer + REACH
    other = device // owners
    within = far_boxes % box_dev
    pieces = []
    for offset in range(-REACH, REACH + 1):
        if offset == 0:
            pieces.append(multipole)
        else:
            pieces.append(from_behind(multipole, "box", -offset))
    window = lax.all_gather(jnp.stack(pieces)[None], "group", axis=0, tiled=True)
    location = (other * span + stride) * box_dev + within
    flat = window.reshape(-1, 3 * NTERM)
    listing = lax.broadcasted_iota(jnp.int32, far_boxes.shape, 1)
    weights = far_scale * (listing < far_count[:, None]).astype(jnp.float32)
    classes = (far_class[:, :, None] == lax.broadcasted_iota(jnp.int32, (1, 1, CLASSES), 2)).astype(
        jnp.float32
    ) * weights[:, :, None]
    matches = (
        location[:, :, None] == lax.broadcasted_iota(jnp.int32, (1, 1, flat.shape[0]), 2)
    ).astype(jnp.float32)
    selector = jnp.einsum("kjo,kjn->kon", classes, matches, precision=HIGH)
    summed = jnp.einsum("kon,nq->koq", selector, flat, precision=HIGH).reshape(
        box_dev, CLASSES, 3, NTERM
    )
    local = jnp.einsum("kocu,otu->kct", summed, translations, precision=HIGH)
    return jnp.einsum("tks,kct->cks", mono_b, local, precision=HIGH).reshape(3, -1)


def on_device(
    dipoles,
    perm_field,
    positions,
    polarizability,
    occupancy,
    far_boxes,
    far_class,
    far_count,
    far_scale,
    translations,
):
    box_dev = occupancy.shape[0]
    slot = lax.broadcasted_iota(jnp.int32, (box_dev, TILE), 1)
    live_mask = (slot < occupancy[:, None]).astype(jnp.float32).reshape(-1)
    source = dipoles * live_mask
    root_pol = lax.rsqrt(polarizability)
    geometry = jnp.concatenate([positions, root_pol[None]], axis=0).reshape(4, 1, FX, FY, TILE)
    neighbours = extended(geometry, (("box", 1),), 1)
    neighbours = jnp.pad(neighbours, ((0, 0), (0, 0), (1, 1), (1, 1), (0, 0)))
    target_rel = positions.reshape(3, box_dev, TILE)
    target_root = root_pol.reshape(box_dev, TILE)
    monomial = monomials(positions)
    far_part = far_field(source, monomial, far_boxes, far_class, far_count, far_scale, translations)
    near_zero = near_operator(source, neighbours, target_rel, target_root)
    residual = live_mask * (perm_field + far_part + near_zero - source / polarizability)
    sweep_one = polarizability * residual
    sweep_two = (
        live_mask
        * polarizability
        * (residual + near_operator(sweep_one, neighbours, target_rel, target_root))
    )
    sweep_three = (
        live_mask
        * polarizability
        * (residual + near_operator(sweep_two, neighbours, target_rel, target_root))
    )
    return (source + sweep_three, residual)


def solution(mesh):
    return jax.shard_map(
        on_device,
        mesh=mesh,
        in_specs=(
            P(None, ("group", "box")),
            P(None, ("group", "box")),
            P(None, ("group", "box")),
            P(("group", "box")),
            P(("group", "box")),
            P(("group", "box"), None),
            P(("group", "box"), None),
            P(("group", "box")),
            P(("group", "box"), None),
            P(),
        ),
        out_specs=(P(None, ("group", "box")), P(None, ("group", "box"))),
        check_vma=False,
    )
```

profile of v0, /device:TPU:11, one launch (start us, length us, event | category | flops | bytes accessed | tf_op | source)
XLA Modules:
  0.0 86.9 jit_solution(2009084336131571979)
XLA Ops:
  2.1 0.9 subtract_multiply_fusion.86
  3.0 0.9 %subtract_multiply_fusion.89 = (f32[1,256]{1,0:T(1,128)S(1)}, f32[1,256]{1,0:T(1,128)S(1)}, f32[1,256]{1,0:T(1,128)S(1)}, f32[1,256]{1,0:T(1,128)S(1)}, f32[1,25...) fusion(f32[3,256]{1,0:T(4,128)} %param.18, ...), kind=kLoop, calls=%fused_computation.825 | loop fusion | flops 37888 | bytes 21504 | tf_op jit(solution)/shard_map/reduce_sum | solution.py:93
  3.8 0.9 %subtract_multiply_fusion.104 = (f32[1,256]{1,0:T(1,128)S(1)}, f32[1,256]{1,0:T(1,128)S(1)}, f32[1,256]{1,0:T(1,128)S(1)}, f32[1,256]{1,0:T(1,128)S(1)}, f32[1,2...) fusion(f32[3,256]{1,0:T(4,128)} %param.18, ...), kind=kLoop, calls=%fused_computation.860 | loop fusion | flops 38656 | bytes 22528 | tf_op jit(solution)/shard_map/reduce_sum | solution.py:93
  5.4 0.9 %subtract_multiply_fusion.107 = (f32[1,256]{1,0:T(1,128)S(1)}, f32[1,256]{1,0:T(1,128)S(1)}, f32[1,256]{1,0:T(1,128)S(1)}, f32[1,256]{1,0:T(1,128)S(1)}, f32[1,2...) fusion(f32[3,256]{1,0:T(4,128)} %param.18, ...), kind=kLoop, calls=%fused_computation.867 | loop fusion | flops 36352 | bytes 21504 | tf_op jit(solution)/shard_map/reduce_sum | solution.py:93
  12.0 3.2 %collective-permute-start = (f32[2,495]{1,0:T(2,128)S(1)}, f32[2,495]{1,0:T(2,128)S(1)}, u32[]{:S(2)}, u32[]{:S(2)}) collective-permute-start(f32[2,495]{1,0:T(2,128)S(1)} %reshape.1014), channel_id=1, source_target_pairs={{0,4},{1,5},{2,6},{3,7},{4,8},{5,9},{6,10},{7,11},{8,12},{9,13},{1... | collective-permute-start | bytes 11888 | tf_op jit(solution)/shard_map/ppermute | solution.py:38
  15.2 4.0 %collective-permute-start.1 = (f32[2,495]{1,0:T(2,128)S(1)}, f32[2,495]{1,0:T(2,128)S(1)}, u32[]{:S(2)}, u32[]{:S(2)}) collective-permute-start(f32[2,495]{1,0:T(2,128)S(1)} %reshape.1014), channel_id=1, source_target_pairs={{0,3},{1,4},{2,5},{3,6},{4,7},{5,8},{6,9},{7,10},{8,11},{9,12},{10... | collective-permute-start | bytes 11888 | tf_op jit(solution)/shard_map/ppermute | solution.py:38
  19.2 1.9 %collective-permute-start.2 = (f32[2,495]{1,0:T(2,128)S(1)}, f32[2,495]{1,0:T(2,128)S(1)}, u32[]{:S(2)}, u32[]{:S(2)}) collective-permute-start(f32[2,495]{1,0:T(2,128)S(1)} %reshape.1014), channel_id=1, source_target_pairs={{0,2},{1,3},{2,4},{3,5},{4,6},{5,7},{6,8},{7,9},{8,10},{9,11},{10,... | collective-permute-start | bytes 11888 | tf_op jit(solution)/shard_map/ppermute | solution.py:38
  21.2 3.4 %collective-permute-start.10 = (f32[3,1,2,1,128]{4,2,3,1,0:T(2,128)S(1)}, f32[3,1,2,1,128]{4,2,3,1,0:T(2,128)S(1)}, u32[]{:S(2)}, u32[]{:S(2)}) collective-permute-start(f32[3,1,2,1,128]{4,2,3,1,0:T(2,128)S(1)} %bitcast.518), channel_id=1, source_target_pairs={{0,1},{1,2},{2,3},{3,4},{4,5},{5,6},{6,7},{7,8},{8,9},{9,10},{10,1... | collective-permute-start | bytes 9224 | tf_op jit(solution)/shard_map/ppermute | solution.py:27
  24.5 1.9 %collective-permute-start.11 = (f32[3,1,2,1,128]{4,2,3,1,0:T(2,128)S(1)}, f32[3,1,2,1,128]{4,2,3,1,0:T(2,128)S(1)}, u32[]{:S(2)}, u32[]{:S(2)}) collective-permute-start(f32[3,1,2,1,128]{4,2,3,1,0:T(2,128)S(1)} %bitcast.519), channel_id=1, source_target_pairs={{1,0},{2,1},{3,2},{4,3},{5,4},{6,5},{7,6},{8,7},{9,8},{10,9},{11,1... | collective-permute-start | bytes 9224 | tf_op jit(solution)/shard_map/ppermute | solution.py:30
  27.6 4.5 %collective-permute-start.3 = (f32[2,495]{1,0:T(2,128)S(1)}, f32[2,495]{1,0:T(2,128)S(1)}, u32[]{:S(2)}, u32[]{:S(2)}) collective-permute-start(f32[2,495]{1,0:T(2,128)S(1)} %reshape.1014), channel_id=1, source_target_pairs={{0,1},{1,2},{2,3},{3,4},{4,5},{5,6},{6,7},{7,8},{8,9},{9,10},{10,1... | collective-permute-start | bytes 11888 | tf_op jit(solution)/shard_map/ppermute | solution.py:38
  32.1 1.9 %collective-permute-start.4 = (f32[2,495]{1,0:T(2,128)S(1)}, f32[2,495]{1,0:T(2,128)S(1)}, u32[]{:S(2)}, u32[]{:S(2)}) collective-permute-start(f32[2,495]{1,0:T(2,128)S(1)} %reshape.1014), channel_id=1, source_target_pairs={{1,0},{2,1},{3,2},{4,3},{5,4},{6,5},{7,6},{8,7},{9,8},{10,9},{11,1... | collective-permute-start | bytes 11888 | tf_op jit(solution)/shard_map/ppermute | solution.py:38
  34.2 1.9 %collective-permute-start.5 = (f32[2,495]{1,0:T(2,128)S(1)}, f32[2,495]{1,0:T(2,128)S(1)}, u32[]{:S(2)}, u32[]{:S(2)}) collective-permute-start(f32[2,495]{1,0:T(2,128)S(1)} %reshape.1014), channel_id=1, source_target_pairs={{2,0},{3,1},{4,2},{5,3},{6,4},{7,5},{8,6},{9,7},{10,8},{11,9},{12,... | collective-permute-start | bytes 11888 | tf_op jit(solution)/shard_map/ppermute | solution.py:38
  36.1 4.2 %collective-permute-start.6 = (f32[2,495]{1,0:T(2,128)S(1)}, f32[2,495]{1,0:T(2,128)S(1)}, u32[]{:S(2)}, u32[]{:S(2)}) collective-permute-start(f32[2,495]{1,0:T(2,128)S(1)} %reshape.1014), channel_id=1, source_target_pairs={{3,0},{4,1},{5,2},{6,3},{7,4},{8,5},{9,6},{10,7},{11,8},{12,9},{13... | collective-permute-start | bytes 11888 | tf_op jit(solution)/shard_map/ppermute | solution.py:38
  40.4 1.9 %collective-permute-start.7 = (f32[2,495]{1,0:T(2,128)S(1)}, f32[2,495]{1,0:T(2,128)S(1)}, u32[]{:S(2)}, u32[]{:S(2)}) collective-permute-start(f32[2,495]{1,0:T(2,128)S(1)} %reshape.1014), channel_id=1, source_target_pairs={{4,0},{5,1},{6,2},{7,3},{8,4},{9,5},{10,6},{11,7},{12,8},{13,9},{1... | collective-permute-start | bytes 11888 | tf_op jit(solution)/shard_map/ppermute | solution.py:38
  42.3 3.4 %collective-permute-start.8 = (f32[4,1,2,1,128]{4,2,0,3,1:T(2,128)S(1)}, f32[4,1,2,1,128]{4,2,0,3,1:T(2,128)S(1)}, u32[]{:S(2)}, u32[]{:S(2)}) collective-permute-start(f32[4,1,2,1,128]{4,2,0,3,1:T(2,128)S(1)} %pad_maximum_fusion.1), channel_id=1, source_target_pairs={{0,1},{1,2},{2,3},{3,4},{4,5},{5,6},{6,7},{7,8},{8,9},{9,10},{10,1... | collective-permute-start | bytes 12296 | tf_op jit(solution)/shard_map/ppermute | solution.py:27
  45.7 1.9 %collective-permute-start.9 = (f32[4,1,2,1,128]{4,2,0,3,1:T(2,128)S(1)}, f32[4,1,2,1,128]{4,2,0,3,1:T(2,128)S(1)}, u32[]{:S(2)}, u32[]{:S(2)}) collective-permute-start(f32[4,1,2,1,128]{4,2,0,3,1:T(2,128)S(1)} %pad_maximum_fusion.1), channel_id=1, source_target_pairs={{1,0},{2,1},{3,2},{4,3},{5,4},{6,5},{7,6},{8,7},{9,8},{10,9},{11,1... | collective-permute-start | bytes 12296 | tf_op jit(solution)/shard_map/ppermute | solution.py:30
  47.7 3.5 %all-gather = f32[18,2,495]{2,1,0:T(2,128)S(1)} all-gather(f32[9,2,495]{2,1,0:T(2,128)S(1)} %constant_dynamic-update-slice_fusion), channel_id=2, replica_groups=mesh['group'=2,'box'=16] {'group'}, dimensions={0}, use_global_device_ids=true | all-gather | bytes 106920 | tf_op jit(solution)/shard_map/all_gather | solution.py:150
  51.6 1.6 %fusion.3 = f32[2,3,165]{2,1,0:T(4,128)S(1)} fusion(f32[8,165,165]{2,0,1:T(8,128)S(1)} %copy-done, f32[2,8,3,165]{3,1,2,0:T(8,128)S(1)} %fusion.291), kind=kOutput, calls=%fused_computation.6 | convolution fusion | flops 15681600 | bytes 906840 | tf_op jit(solution)/shard_map/kocu,otu->kct/dot_general | solution.py:165
  58.0 5.7 %collective-permute-start.12 = (f32[3,1,2,1,128]{4,2,3,1,0:T(2,128)S(1)}, f32[3,1,2,1,128]{4,2,3,1,0:T(2,128)S(1)}, u32[]{:S(2)}, u32[]{:S(2)}) collective-permute-start(f32[3,1,2,1,128]{4,2,3,1,0:T(2,128)S(1)} %bitcast.524), channel_id=1, source_target_pairs={{0,1},{1,2},{2,3},{3,4},{4,5},{5,6},{6,7},{7,8},{8,9},{9,10},{10,1... | collective-permute-start | bytes 9224 | tf_op jit(solution)/shard_map/ppermute | solution.py:27
  63.7 2.1 %collective-permute-start.13 = (f32[3,1,2,1,128]{4,2,3,1,0:T(2,128)S(1)}, f32[3,1,2,1,128]{4,2,3,1,0:T(2,128)S(1)}, u32[]{:S(2)}, u32[]{:S(2)}) collective-permute-start(f32[3,1,2,1,128]{4,2,3,1,0:T(2,128)S(1)} %bitcast.525), channel_id=1, source_target_pairs={{1,0},{2,1},{3,2},{4,3},{5,4},{6,5},{7,6},{8,7},{9,8},{10,9},{11,1... | collective-permute-start | bytes 9224 | tf_op jit(solution)/shard_map/ppermute | solution.py:30
  66.3 3.1 %collective-permute-done.13 = f32[3,1,2,1,128]{4,2,3,1,0:T(2,128)S(1)} collective-permute-done((f32[3,1,2,1,128]{4,2,3,1,0:T(2,128)S(1)}, f32[3,1,2,1,128]{4,2,3,1,0:T(2,128)S(1)}, u32[]{:S(2)}, u32[]{:S(2)}) %collective-permute-start.13) | collective-permute-done | bytes 3104 | tf_op jit(solution)/shard_map/ppermute | solution.py:30
  74.0 1.9 %collective-permute-start.14 = (f32[3,1,2,1,128]{4,2,3,1,0:T(2,128)S(1)}, f32[3,1,2,1,128]{4,2,3,1,0:T(2,128)S(1)}, u32[]{:S(2)}, u32[]{:S(2)}) collective-permute-start(f32[3,1,2,1,128]{4,2,3,1,0:T(2,128)S(1)} %bitcast.521), channel_id=1, source_target_pairs={{0,1},{1,2},{2,3},{3,4},{4,5},{5,6},{6,7},{7,8},{8,9},{9,10},{10,1... | collective-permute-start | bytes 9224 | tf_op jit(solution)/shard_map/ppermute | solution.py:27
  76.0 2.4 %collective-permute-start.15 = (f32[3,1,2,1,128]{4,2,3,1,0:T(2,128)S(1)}, f32[3,1,2,1,128]{4,2,3,1,0:T(2,128)S(1)}, u32[]{:S(2)}, u32[]{:S(2)}) collective-permute-start(f32[3,1,2,1,128]{4,2,3,1,0:T(2,128)S(1)} %bitcast.522), channel_id=1, source_target_pairs={{1,0},{2,1},{3,2},{4,3},{5,4},{6,5},{7,6},{8,7},{9,8},{10,9},{11,1... | collective-permute-start | bytes 9224 | tf_op jit(solution)/shard_map/ppermute | solution.py:30
  78.9 2.9 %collective-permute-done.15 = f32[3,1,2,1,128]{4,2,3,1,0:T(2,128)S(1)} collective-permute-done((f32[3,1,2,1,128]{4,2,3,1,0:T(2,128)S(1)}, f32[3,1,2,1,128]{4,2,3,1,0:T(2,128)S(1)}, u32[]{:S(2)}, u32[]{:S(2)}) %collective-permute-start.15) | collective-permute-done | bytes 3104 | tf_op jit(solution)/shard_map/ppermute | solution.py:30
  (145 shorter events, 24.5 us)
Async XLA Ops:
  10.4 16.0 %copy-start.1 = (f32[3,256]{1,0:T(4,128)S(1)}, f32[3,256]{1,0:T(4,128)}, u32[]{:S(2)}) copy-start(f32[3,256]{1,0:T(4,128)} %param.18) | copy-start | bytes 9220
  10.4 16.1 %copy-start.4 = (s32[2,189]{1,0:T(2,128)S(1)}, s32[2,189]{1,0:T(2,128)}, u32[]{:S(2)}) copy-start(s32[2,189]{1,0:T(2,128)} %param.21) | copy-start | bytes 4540
  10.5 16.1 %copy-start.5 = (f32[2,189]{1,0:T(2,128)S(1)}, f32[2,189]{1,0:T(2,128)}, u32[]{:S(2)}) copy-start(f32[2,189]{1,0:T(2,128)} %param.24) | copy-start | bytes 4540
  10.5 16.1 %copy-start.7 = (s32[2]{0:T(128)S(1)}, s32[2]{0:T(128)}, u32[]{:S(2)}) copy-start(s32[2]{0:T(128)} %param.23) | copy-start | bytes 28
  10.5 16.2 %copy-start.9 = (s32[2,189]{1,0:T(2,128)S(1)}, s32[2,189]{1,0:T(2,128)}, u32[]{:S(2)}) copy-start(s32[2,189]{1,0:T(2,128)} %param.22) | copy-start | bytes 4540
  11.3 40.3 %copy-start = (f32[8,165,165]{2,0,1:T(8,128)S(1)}, f32[8,165,165]{2,0,1:T(8,128)}, u32[]{:S(2)}) copy-start(f32[8,165,165]{2,0,1:T(8,128)} %param.25) | copy-start | bytes 2613604
  12.0 22.2 %collective-permute-start = (f32[2,495]{1,0:T(2,128)S(1)}, f32[2,495]{1,0:T(2,128)S(1)}, u32[]{:S(2)}, u32[]{:S(2)}) collective-permute-start(f32[2,495]{1,0:T(2,128)S(1)} %reshape.1014), channel_id=1, source_target_pairs={{0,4},{1,5},{2,6},{3,7},{4,8},{5,9},{6,10},{7,11},{8,12},{9,13},{1... | collective-permute-start | bytes 11888 | tf_op jit(solution)/shard_map/ppermute | solution.py:38
  15.2 20.9 %collective-permute-start.1 = (f32[2,495]{1,0:T(2,128)S(1)}, f32[2,495]{1,0:T(2,128)S(1)}, u32[]{:S(2)}, u32[]{:S(2)}) collective-permute-start(f32[2,495]{1,0:T(2,128)S(1)} %reshape.1014), channel_id=1, source_target_pairs={{0,3},{1,4},{2,5},{3,6},{4,7},{5,8},{6,9},{7,10},{8,11},{9,12},{10... | collective-permute-start | bytes 11888 | tf_op jit(solution)/shard_map/ppermute | solution.py:38
  19.2 21.1 %collective-permute-start.2 = (f32[2,495]{1,0:T(2,128)S(1)}, f32[2,495]{1,0:T(2,128)S(1)}, u32[]{:S(2)}, u32[]{:S(2)}) collective-permute-start(f32[2,495]{1,0:T(2,128)S(1)} %reshape.1014), channel_id=1, source_target_pairs={{0,2},{1,3},{2,4},{3,5},{4,6},{5,7},{6,8},{7,9},{8,10},{9,11},{10,... | collective-permute-start | bytes 11888 | tf_op jit(solution)/shard_map/ppermute | solution.py:38
  21.2 6.4 %collective-permute-start.10 = (f32[3,1,2,1,128]{4,2,3,1,0:T(2,128)S(1)}, f32[3,1,2,1,128]{4,2,3,1,0:T(2,128)S(1)}, u32[]{:S(2)}, u32[]{:S(2)}) collective-permute-start(f32[3,1,2,1,128]{4,2,3,1,0:T(2,128)S(1)} %bitcast.518), channel_id=1, source_target_pairs={{0,1},{1,2},{2,3},{3,4},{4,5},{5,6},{6,7},{7,8},{8,9},{9,10},{10,1... | collective-permute-start | bytes 9224 | tf_op jit(solution)/shard_map/ppermute | solution.py:27
  24.5 7.6 %collective-permute-start.11 = (f32[3,1,2,1,128]{4,2,3,1,0:T(2,128)S(1)}, f32[3,1,2,1,128]{4,2,3,1,0:T(2,128)S(1)}, u32[]{:S(2)}, u32[]{:S(2)}) collective-permute-start(f32[3,1,2,1,128]{4,2,3,1,0:T(2,128)S(1)} %bitcast.519), channel_id=1, source_target_pairs={{1,0},{2,1},{3,2},{4,3},{5,4},{6,5},{7,6},{8,7},{9,8},{10,9},{11,1... | collective-permute-start | bytes 9224 | tf_op jit(solution)/shard_map/ppermute | solution.py:30
  27.6 14.8 %collective-permute-start.3 = (f32[2,495]{1,0:T(2,128)S(1)}, f32[2,495]{1,0:T(2,128)S(1)}, u32[]{:S(2)}, u32[]{:S(2)}) collective-permute-start(f32[2,495]{1,0:T(2,128)S(1)} %reshape.1014), channel_id=1, source_target_pairs={{0,1},{1,2},{2,3},{3,4},{4,5},{5,6},{6,7},{7,8},{8,9},{9,10},{10,1... | collective-permute-start | bytes 11888 | tf_op jit(solution)/shard_map/ppermute | solution.py:38
  32.1 13.6 %collective-permute-start.4 = (f32[2,495]{1,0:T(2,128)S(1)}, f32[2,495]{1,0:T(2,128)S(1)}, u32[]{:S(2)}, u32[]{:S(2)}) collective-permute-start(f32[2,495]{1,0:T(2,128)S(1)} %reshape.1014), channel_id=1, source_target_pairs={{1,0},{2,1},{3,2},{4,3},{5,4},{6,5},{7,6},{8,7},{9,8},{10,9},{11,1... | collective-permute-start | bytes 11888 | tf_op jit(solution)/shard_map/ppermute | solution.py:38
  34.2 13.5 %collective-permute-start.5 = (f32[2,495]{1,0:T(2,128)S(1)}, f32[2,495]{1,0:T(2,128)S(1)}, u32[]{:S(2)}, u32[]{:S(2)}) collective-permute-start(f32[2,495]{1,0:T(2,128)S(1)} %reshape.1014), channel_id=1, source_target_pairs={{2,0},{3,1},{4,2},{5,3},{6,4},{7,5},{8,6},{9,7},{10,8},{11,9},{12,... | collective-permute-start | bytes 11888 | tf_op jit(solution)/shard_map/ppermute | solution.py:38
  36.1 11.6 %collective-permute-start.6 = (f32[2,495]{1,0:T(2,128)S(1)}, f32[2,495]{1,0:T(2,128)S(1)}, u32[]{:S(2)}, u32[]{:S(2)}) collective-permute-start(f32[2,495]{1,0:T(2,128)S(1)} %reshape.1014), channel_id=1, source_target_pairs={{3,0},{4,1},{5,2},{6,3},{7,4},{8,5},{9,6},{10,7},{11,8},{12,9},{13... | collective-permute-start | bytes 11888 | tf_op jit(solution)/shard_map/ppermute | solution.py:38
  40.4 7.4 %collective-permute-start.7 = (f32[2,495]{1,0:T(2,128)S(1)}, f32[2,495]{1,0:T(2,128)S(1)}, u32[]{:S(2)}, u32[]{:S(2)}) collective-permute-start(f32[2,495]{1,0:T(2,128)S(1)} %reshape.1014), channel_id=1, source_target_pairs={{4,0},{5,1},{6,2},{7,3},{8,4},{9,5},{10,6},{11,7},{12,8},{13,9},{1... | collective-permute-start | bytes 11888 | tf_op jit(solution)/shard_map/ppermute | solution.py:38
  42.3 10.9 %collective-permute-start.8 = (f32[4,1,2,1,128]{4,2,0,3,1:T(2,128)S(1)}, f32[4,1,2,1,128]{4,2,0,3,1:T(2,128)S(1)}, u32[]{:S(2)}, u32[]{:S(2)}) collective-permute-start(f32[4,1,2,1,128]{4,2,0,3,1:T(2,128)S(1)} %pad_maximum_fusion.1), channel_id=1, source_target_pairs={{0,1},{1,2},{2,3},{3,4},{4,5},{5,6},{6,7},{7,8},{8,9},{9,10},{10,1... | collective-permute-start | bytes 12296 | tf_op jit(solution)/shard_map/ppermute | solution.py:27
  45.7 7.5 %collective-permute-start.9 = (f32[4,1,2,1,128]{4,2,0,3,1:T(2,128)S(1)}, f32[4,1,2,1,128]{4,2,0,3,1:T(2,128)S(1)}, u32[]{:S(2)}, u32[]{:S(2)}) collective-permute-start(f32[4,1,2,1,128]{4,2,0,3,1:T(2,128)S(1)} %pad_maximum_fusion.1), channel_id=1, source_target_pairs={{1,0},{2,1},{3,2},{4,3},{5,4},{6,5},{7,6},{8,7},{9,8},{10,9},{11,1... | collective-permute-start | bytes 12296 | tf_op jit(solution)/shard_map/ppermute | solution.py:30
  53.3 4.4 %copy-start.8 = (f32[3,256]{1,0:T(4,128)S(1)}, f32[3,256]{1,0:T(4,128)}, u32[]{:S(2)}) copy-start(f32[3,256]{1,0:T(4,128)} %param.17) | copy-start | bytes 9220
  57.9 28.2 %copy-start.2 = (f32[3,256]{1,0:T(4,128)}, f32[3,256]{1,0:T(4,128)S(1)}, u32[]{:S(2)}) copy-start(f32[3,256]{1,0:T(4,128)S(1)} %get-tuple-element.488) | copy-start | bytes 9220
  58.0 8.4 %collective-permute-start.12 = (f32[3,1,2,1,128]{4,2,3,1,0:T(2,128)S(1)}, f32[3,1,2,1,128]{4,2,3,1,0:T(2,128)S(1)}, u32[]{:S(2)}, u32[]{:S(2)}) collective-permute-start(f32[3,1,2,1,128]{4,2,3,1,0:T(2,128)S(1)} %bitcast.524), channel_id=1, source_target_pairs={{0,1},{1,2},{2,3},{3,4},{4,5},{5,6},{6,7},{7,8},{8,9},{9,10},{10,1... | collective-permute-start | bytes 9224 | tf_op jit(solution)/shard_map/ppermute | solution.py:27
  63.7 5.8 %collective-permute-start.13 = (f32[3,1,2,1,128]{4,2,3,1,0:T(2,128)S(1)}, f32[3,1,2,1,128]{4,2,3,1,0:T(2,128)S(1)}, u32[]{:S(2)}, u32[]{:S(2)}) collective-permute-start(f32[3,1,2,1,128]{4,2,3,1,0:T(2,128)S(1)} %bitcast.525), channel_id=1, source_target_pairs={{1,0},{2,1},{3,2},{4,3},{5,4},{6,5},{7,6},{8,7},{9,8},{10,9},{11,1... | collective-permute-start | bytes 9224 | tf_op jit(solution)/shard_map/ppermute | solution.py:30
  74.0 4.9 %collective-permute-start.14 = (f32[3,1,2,1,128]{4,2,3,1,0:T(2,128)S(1)}, f32[3,1,2,1,128]{4,2,3,1,0:T(2,128)S(1)}, u32[]{:S(2)}, u32[]{:S(2)}) collective-permute-start(f32[3,1,2,1,128]{4,2,3,1,0:T(2,128)S(1)} %bitcast.521), channel_id=1, source_target_pairs={{0,1},{1,2},{2,3},{3,4},{4,5},{5,6},{6,7},{7,8},{8,9},{9,10},{10,1... | collective-permute-start | bytes 9224 | tf_op jit(solution)/shard_map/ppermute | solution.py:27
  76.0 5.8 %collective-permute-start.15 = (f32[3,1,2,1,128]{4,2,3,1,0:T(2,128)S(1)}, f32[3,1,2,1,128]{4,2,3,1,0:T(2,128)S(1)}, u32[]{:S(2)}, u32[]{:S(2)}) collective-permute-start(f32[3,1,2,1,128]{4,2,3,1,0:T(2,128)S(1)} %bitcast.522), channel_id=1, source_target_pairs={{1,0},{2,1},{3,2},{4,3},{5,4},{6,5},{7,6},{8,7},{9,8},{10,9},{11,1... | collective-permute-start | bytes 9224 | tf_op jit(solution)/shard_map/ppermute | solution.py:30
  (2 other events, 5.4 us)
where the time goes:
time: 88 us; the launch traced here: 86.9 us
  starting transfers between devices  46.4 us (53%)
  other arithmetic  23.6 us (27%)
  waiting for transfers between devices  6.03 us (7%)
  blocking collectives  3.49 us (4%)
  local copies, waits for them, and re-layouts  3.34 us (4%)
  matrix products  2.63 us (3%)
  between operations  1.46 us (2%)
    ppermute x8, starting transfers between devices, from_behind(): return lax.ppermute(x, axis, pairs)  23.7 us
    reduce_sum x37, other arithmetic, pair_field(): jnp.sum(deltas[component] * radial - direct * source_dip[component][:, No...  19.4 us
    ppermute x4, starting transfers between devices, extended(): lax.ppermute(lax.slice_in_dim(block, block.shape[dim] - width, None, axis...  14.4 us
    ppermute x4, starting transfers between devices, extended(): lax.ppermute(lax.slice_in_dim(block, 0, width, axis=dim), axis, backward)  8.32 us
    ppermute x4, waiting for transfers between devices, extended(): lax.ppermute(lax.slice_in_dim(block, 0, width, axis=dim), axis, backward)  5.99 us
    all_gather x1, blocking collectives, far_field(): lax.all_gather(jnp.stack(pieces)[None], 'group', axis=0, tiled=True)  3.49 us
    gather x3, local copies, waits for them, and re-layouts, monomials(): return cheb_x[table[:, 0]] * cheb_y[table[:, 1]] * cheb_z[table[:, 2]]  2.47 us
  transfers between devices with their start and end apart: 16, of which 2 were waited for; matrix products, arithmetic and copies ran while one was open for 5% of the time, Pallas kernels for 0%

commit v1 on v0

v1 whole, which is shorter than its diff:
```python
import functools
import jax
import jax.numpy as jnp
import numpy as np
from jax import lax
from jax.experimental import pallas as pl
from jax.experimental.pallas import tpu as pltpu
from jax.sharding import PartitionSpec as P

TILE = 128
ORDER = 8
FX = 2
FY = 1
REACH = 4
SPAN = 2 * REACH + 1
WIDE = 256
ROWS = 16

HALF = 5.4
THOLE = 0.39
SOFT = 1.0
MESH = pl.DeviceIdType.MESH
F32 = jnp.float32
BF16 = jnp.bfloat16
LANES = (((1,), (1,)), ((), ()))
PLAIN = (((1,), (0,)), ((), ()))


def term_table(order):
    listing = []
    for degree in range(order + 1):
        for first_idx in range(degree + 1):
            for second_idx in range(degree + 1 - first_idx):
                listing.append((first_idx, second_idx, degree - first_idx - second_idx))
    return np.array(listing, dtype=np.int32)


def pick_matrix():
    table = term_table(ORDER)
    pick = np.zeros((3, WIDE, 64), np.float32)
    for term, powers in enumerate(table):
        for axis in range(3):
            for part in range(2):
                pick[axis, term, 32 * part + 3 * powers[axis] + axis] = 1.0
    return pick.reshape(3 * WIDE, 64)


def split(x):
    high = x.astype(BF16)
    return high, (x - high.astype(F32)).astype(BF16)


def dot(a, b, dims):
    return lax.dot_general(a, b, dims, preferred_element_type=F32)


def dot_parts(a, b, dims):
    return dot(a[0], b[0], dims) + (dot(a[0], b[1], dims) + dot(a[1], b[0], dims))


def kernel(
    groups, owners,
    dip_ref, perm_ref, pos_ref, pol_ref, occ_ref, fbox_ref, fcls_ref, fcnt_ref, fscl_ref,
    trans_ref, pick_ref,
    new_ref, res_ref,
    own, beside, geo_t, mono_ref, window, tensor, acc,
    nsend, nrecv, wsend, wrecv,
):
    group = lax.axis_index("group")
    layer = lax.axis_index("box")

    def in_range(step):
        place = layer + step
        return jnp.logical_and(place >= 0, place < owners)

    def neighbour(step):
        return jnp.clip(layer + step, 0, owners - 1)

    def far_peers(act):
        for peer_group in range(groups):
            for step in range(-REACH, REACH + 1):
                ok = in_range(step) if step else group != peer_group
                pl.when(ok)(functools.partial(act, peer_group, step))

    barrier = pltpu.get_barrier_semaphore()

    def greet(peer_group, step):
        pl.semaphore_signal(
            barrier, inc=1, device_id=(peer_group, neighbour(step)), device_id_type=MESH
        )

    far_peers(greet)

    for step in range(-REACH, REACH + 1):
        if step:

            @pl.when(jnp.logical_not(in_range(step)))
            def _(step=step):
                for peer_group in range(groups):
                    window[peer_group * SPAN + step + REACH] = jnp.zeros((8, WIDE), F32)

    for side, step in enumerate((-1, 1)):

        @pl.when(jnp.logical_not(in_range(step)))
        def _(side=side):
            for turn in range(3):
                beside[turn, side] = jnp.zeros((8, WIDE), F32)

    lane = lax.broadcasted_iota(jnp.int32, (1, 2 * TILE), 1)
    second = lane >= TILE
    slot = jnp.where(second, lane - TILE, lane)
    live = (slot < jnp.where(second, occ_ref[1:2], occ_ref[0:1])).astype(F32)
    pol = pol_ref[...]
    root = lax.rsqrt(pol)
    pos = pos_ref[...]
    source = dip_ref[...] * live
    place_x = HALF * (pos[0:1] + jnp.where(second, 2.0, 0.0))
    own[0] = jnp.concatenate(
        [place_x, HALF * pos[1:3], root, source, jnp.zeros((1, WIDE), F32)], axis=0
    )
    geo_t[...] = jnp.transpose(own[0])

    series = [jnp.ones_like(pos), pos]
    for _ in range(2, ORDER + 1):
        series.append(2.0 * pos * series[-1] - series[-2])
    cheb = jnp.concatenate(series + [jnp.zeros((5, WIDE), F32)], axis=0)
    planes = dot(pick_ref[...], jnp.concatenate(split(cheb), axis=0), PLAIN)
    mono = planes[0:WIDE] * planes[WIDE : 2 * WIDE] * planes[2 * WIDE :]
    mono_ref[...] = mono
    first_half = jnp.where(second, 0.0, source)
    second_half = source - first_half
    moments = jnp.concatenate([first_half, second_half, jnp.zeros((2, WIDE), F32)], axis=0)
    window[group * SPAN + REACH] = dot_parts(split(moments), split(mono), LANES)

    below = jnp.minimum(layer, REACH)
    above = jnp.minimum(owners - 1 - layer, REACH)
    pl.semaphore_wait(barrier, (below + above + 1) * groups - 1)

    def near_copy(turn, side, step):
        return pltpu.make_async_remote_copy(
            src_ref=own.at[turn],
            dst_ref=beside.at[turn, side],
            send_sem=nsend.at[2 * turn + side],
            recv_sem=nrecv.at[2 * turn + side],
            device_id=(group, neighbour(step)),
            device_id_type=MESH,
        )

    def near_send(turn):
        for side, step in enumerate((1, -1)):
            pl.when(in_range(step))(
                lambda side=side, step=step: near_copy(turn, side, step).start()
            )

    def near_wait(turn):
        for side, step in enumerate((-1, 1)):
            pl.when(in_range(step))(
                lambda side=side, step=step: near_copy(turn, side, step).wait_recv()
            )

    near_send(0)

    def far_send(peer_group, step):
        pltpu.make_async_remote_copy(
            src_ref=window.at[group * SPAN + REACH],
            dst_ref=window.at[group * SPAN + REACH - step],
            send_sem=wsend.at[peer_group * SPAN + REACH + step],
            recv_sem=wrecv.at[group * SPAN + REACH - step],
            device_id=(peer_group, neighbour(step)),
            device_id_type=MESH,
        ).start()

    far_peers(far_send)

    def far_copy(peer_group, step):
        place = peer_group * SPAN + REACH + step
        return pltpu.make_async_remote_copy(
            src_ref=window.at[group * SPAN + REACH],
            dst_ref=window.at[place],
            send_sem=wsend.at[place],
            recv_sem=wrecv.at[place],
            device_id=(peer_group, neighbour(step)),
            device_id_type=MESH,
        )

    def build(number, load, shift):
        def body(block, carry):
            rows = pl.ds(pl.multiple_of(block * ROWS, ROWS), ROWS)
            target = geo_t[rows, :]
            total = [None] * 3
            for half in range(2):
                geo = load(half)
                delta = [target[:, axis : axis + 1] - geo[axis : axis + 1] for axis in range(2)]
                delta.append(target[:, 2:3] - (geo[2:3] + 2.0 * HALF * shift))
                squared = delta[0] * delta[0] + delta[1] * delta[1] + (delta[2] * delta[2] + SOFT)
                inverse = lax.rsqrt(squared)
                strength = squared * squared * inverse * (THOLE * target[:, 3:4] * geo[3:4])
                damping = jnp.exp(-strength)
                lambda_three = 1.0 - damping
                lambda_five = lambda_three - strength * damping
                inverse_two = inverse * inverse
                cube = inverse_two * inverse
                direct = lambda_three * cube
                radial = 3.0 * lambda_five * (cube * inverse_two)
                if number == 0:
                    shape = (ROWS, TILE)
                    here = block * ROWS + lax.broadcasted_iota(jnp.int32, shape, 0)
                    other = half * TILE + lax.broadcasted_iota(jnp.int32, shape, 1)
                    keep = here != other
                    direct = jnp.where(keep, direct, 0.0)
                    radial = jnp.where(keep, radial, 0.0)
                scaled = [radial * part for part in delta]
                entries = [
                    scaled[0] * delta[0] - direct,
                    scaled[1] * delta[1] - direct,
                    scaled[2] * delta[2] - direct,
                    scaled[0] * delta[1],
                    scaled[0] * delta[2],
                    scaled[1] * delta[2],
                ]
                for index, entry in enumerate(entries):
                    tensor[2 * number + half, index, rows, :] = entry
                total = gather(total, entries, [geo[4:5], geo[5:6], geo[6:7]])
            for axis in range(3):
                if number == 0:
                    acc[axis, rows, :] = total[axis]
                else:
                    acc[axis, rows, :] += total[axis]
            return carry

        lax.fori_loop(0, 2 * TILE // ROWS, body, 0)

    def gather(total, m, q):
        terms = [
            m[0] * q[0] + m[3] * q[1] + m[4] * q[2],
            m[3] * q[0] + m[1] * q[1] + m[5] * q[2],
            m[4] * q[0] + m[5] * q[1] + m[2] * q[2],
        ]
        return [t if old is None else old + t for old, t in zip(total, terms)]

    def apply(numbers, rows_of, first):
        parts = [
            [rows_of(number)[axis : axis + 1, half * TILE : (half + 1) * TILE] for axis in range(3)]
            for number in numbers
            for half in range(2)
        ]

        def body(block, carry):
            rows = pl.ds(pl.multiple_of(block * ROWS, ROWS), ROWS)
            total = [None] * 3 if first else [acc[axis, rows, :] for axis in range(3)]
            for place, number in enumerate(numbers):
                for half in range(2):
                    entries = [tensor[2 * number + half, index, rows, :] for index in range(6)]
                    total = gather(total, entries, parts[2 * place + half])
            for axis in range(3):
                acc[axis, rows, :] = total[axis]
            return carry

        lax.fori_loop(0, 2 * TILE // ROWS, body, 0)

    def collect():
        row = lax.broadcasted_iota(jnp.int32, (8, 2 * TILE), 0)
        total = None
        for axis in range(3):
            unit = (row == axis).astype(F32).astype(BF16)
            part = dot(unit, jnp.concatenate(split(acc[axis]), axis=1), LANES)
            total = part if total is None else total + part
        return total[0:3]

    build(0, lambda half: own[0, :, half * TILE : (half + 1) * TILE], 0.0)

    ilist = fbox_ref.shape[1]
    flat_rows = window.shape[0] * 8
    row = lax.broadcasted_iota(jnp.int32, (flat_rows, 1), 0)
    place, inner = row >> 3, row & 7
    owner_group = jnp.zeros_like(place)
    for peer_group in range(1, groups):
        owner_group += (place >= peer_group * SPAN).astype(jnp.int32)
    number = (owner_group * (owners - SPAN) + place + (layer - REACH)) * (FX * FY)
    number = number + (inner >= 3).astype(jnp.int32)
    number = jnp.where(inner < 6, number, -1)
    line = lax.broadcasted_iota(jnp.int32, (64, ilist), 0)
    entry = lax.broadcasted_iota(jnp.int32, (64, ilist), 1)
    selector = None
    for box in range(FX * FY):
        match = (fbox_ref[box : box + 1] == number).astype(F32).astype(BF16)
        inside = line & 7
        mine = jnp.logical_and(inside >= 3 * box, inside < 3 * box + 3)
        mine = jnp.logical_and(mine, entry < fcnt_ref[box : box + 1])
        mine = jnp.logical_and(mine, fcls_ref[box : box + 1] == (line >> 3))
        weights = split(jnp.where(mine, fscl_ref[box : box + 1], 0.0))
        part = dot(weights[0], match, LANES) + dot(weights[1], match, LANES)
        selector = part if selector is None else selector + part
    left = lax.broadcasted_iota(jnp.int32, selector.shape, 0) & 7
    right = lax.broadcasted_iota(jnp.int32, selector.shape, 1) & 7
    left = jnp.where(left >= 3, left - 3, left)
    right = jnp.where(right >= 3, right - 3, right)
    selector = split(jnp.where(left == right, selector, 0.0))

    near_wait(0)
    for side, shift in enumerate((-1.0, 1.0)):
        build(
            side + 1,
            lambda half, side=side: beside[0, side, :, half * TILE : (half + 1) * TILE],
            shift,
        )
    near_zero = collect()

    far_peers(lambda peer_group, step: far_copy(peer_group, step).wait_recv())
    summed = dot_parts(selector, split(window[...].reshape(flat_rows, WIDE)), PLAIN)
    nterm = trans_ref.shape[1]
    local = None
    for index in range(trans_ref.shape[0]):
        part = dot_parts(
            split(summed[8 * index : 8 * index + 8, 0:nterm]), split(trans_ref[index]), LANES
        )
        local = part if local is None else local + part
    spread = dot_parts(split(local), split(mono_ref[0:nterm]), PLAIN)
    far_part = jnp.where(second, spread[3:6], spread[0:3])

    residual = live * (perm_ref[...] + far_part + near_zero - source / pol)
    res_ref[...] = residual
    sweep = pol * residual
    for turn in (1, 2):
        own[turn] = jnp.concatenate([sweep, jnp.zeros((5, WIDE), F32)], axis=0)
        near_send(turn)
        apply((0,), lambda _, turn=turn: own[turn], True)
        near_wait(turn)
        apply((1, 2), lambda number, turn=turn: beside[turn, number - 1], False)
        sweep = live * pol * (residual + collect())
    new_ref[...] = source + sweep

    for turn in range(3):
        for side, step in enumerate((1, -1)):
            pl.when(in_range(step))(
                lambda turn=turn, side=side, step=step: near_copy(turn, side, step).wait_send()
            )
    far_peers(lambda peer_group, step: far_copy(peer_group, step).wait_send())


def solution(mesh):
    groups, owners = mesh.shape["group"], mesh.shape["box"]

    def on_device(dip, perm, pos, pol, occ, fbox, fcls, fcnt, fscl, trans):
        vmem = pl.BlockSpec(memory_space=pltpu.VMEM)
        slots = groups * SPAN
        return pl.pallas_call(
            functools.partial(kernel, groups, owners),
            out_shape=(jax.ShapeDtypeStruct(dip.shape, F32),) * 2,
            in_specs=[vmem] * 11,
            out_specs=(vmem, vmem),
            scratch_shapes=[
                pltpu.VMEM((3, 8, WIDE), F32),
                pltpu.VMEM((3, 2, 8, WIDE), F32),
                pltpu.VMEM((WIDE, 8), F32),
                pltpu.VMEM((WIDE, WIDE), F32),
                pltpu.VMEM((slots, 8, WIDE), F32),
                pltpu.VMEM((6, 6, 2 * TILE, TILE), F32),
                pltpu.VMEM((3, 2 * TILE, TILE), F32),
                pltpu.SemaphoreType.DMA((6,)),
                pltpu.SemaphoreType.DMA((6,)),
                pltpu.SemaphoreType.DMA((slots,)),
                pltpu.SemaphoreType.DMA((slots,)),
            ],
            compiler_params=pltpu.CompilerParams(
                collective_id=0, has_side_effects=True, vmem_limit_bytes=40 * 1024 * 1024
            ),
        )(
            dip, perm, pos, pol.reshape(1, -1), occ.reshape(-1, 1), fbox, fcls, fcnt.reshape(-1, 1),
            fscl, trans,
            jnp.asarray(pick_matrix(), BF16),
        )

    split_dim = ("group", "box")
    return jax.shard_map(
        on_device,
        mesh=mesh,
        in_specs=(
            P(None, split_dim), P(None, split_dim), P(None, split_dim), P(split_dim),
            P(split_dim), P(split_dim, None), P(split_dim, None), P(split_dim),
            P(split_dim, None), P(),
        ),
        out_specs=(P(None, split_dim), P(None, split_dim)),
        check_vma=False,
    )
```

time: 88 us -> 24.5 us (0.28)
  starting transfers between devices: 46.4 us -> 0 us
  other arithmetic: 23.6 us -> 0 us
  Pallas kernels: 0 us -> 19 us
  waiting for transfers between devices: 6.03 us -> 0 us
  blocking collectives: 3.49 us -> 0 us
  matrix products: 2.63 us -> 0 us
  local copies, waits for them, and re-layouts: 3.34 us -> 4.6 us
    ppermute x16 -> x0, starting transfers between devices: 46.4 us -> none  [the longest x8 23.7 us: from_behind(): return lax.ppermute(x, axis, pairs)]
    reduce_sum x37 -> x0, other arithmetic: 19.4 us -> none  [pair_field(): jnp.sum(deltas[component] * radial - direct * source_dip[component][:, No...]
    pallas_call x0 -> x1, Pallas kernels: none -> 19 us  [on_device(): pl.pallas_call(functools.partial(kernel, groups, owners), out_shape=(jax....]
    ppermute x16 -> x0, waiting for transfers between devices: 6.03 us -> none  [the longest x4 5.99 us: extended(): lax.ppermute(lax.slice_in_dim(block, 0, width, axis=dim), axis, backward)]
    all_gather x1 -> x0, blocking collectives: 3.49 us -> none  [far_field(): lax.all_gather(jnp.stack(pieces)[None], 'group', axis=0, tiled=True)]
    unnamed x28 -> x19, local copies, waits for them, and re-layouts: 0.12 us -> 2.99 us
    dot_general x5 -> x0, matrix products: 2.63 us -> none  [the longest x1 1.61 us: far_field(): local = jnp.einsum('kocu,otu->kct', summed, translations, precision=HIGH)]
    gather x3 -> x0, local copies, waits for them, and re-layouts: 2.47 us -> none  [monomials(): return cheb_x[table[:, 0]] * cheb_y[table[:, 1]] * cheb_z[table[:, 2]]]
  transfers between devices with their start and end apart: 16 -> 0, of which waited for: 2 -> 0; matrix products, arithmetic and copies ran while one was open for 5% -> 0% of each run, Pallas kernels for 0% -> 0%
where the time goes in v1:
time: 24.5 us; the launch traced here: 24.3 us
  Pallas kernels  19 us (78%)
  local copies, waits for them, and re-layouts  4.6 us (19%)
  between operations  0.77 us (3%)
    pallas_call x1, Pallas kernels, on_device(): pl.pallas_call(functools.partial(kernel, groups, owners), out_shape=(jax....  19 us
    unnamed x19, local copies, waits for them, and re-layouts  2.99 us
    reshape x1, local copies, waits for them, and re-layouts, on_device(): occ.reshape(-1, 1)  0.87 us
    reshape x1, local copies, waits for them, and re-layouts, on_device(): fcnt.reshape(-1, 1)  0.74 us

profile of v1, /device:TPU:11, one launch (start us, length us, event | category | flops | bytes accessed | tf_op | source)
XLA Modules:
  0.0 24.3 jit_solution(3636828613753801557)
XLA Ops:
  0.6 0.0 copy-start
  0.6 0.0 copy-start.6
  0.7 0.0 copy-start.5
  0.7 0.0 copy-start.4
  0.7 0.0 copy-start.7
  0.7 0.0 copy-start.3
  0.7 0.0 copy-start.2
  0.7 0.0 copy-start.1
  0.7 0.9 %copy.13.occ_ref = s32[2,1]{1,0:T(2,128)S(1)} copy(s32[2,1]{0,1:T(1,128)} %bitcast.4) | data formatting | bytes 16 | tf_op jit(solution)/shard_map/reshape | solution.py:369
  1.6 0.7 %copy.14.fcnt_ref = s32[2,1]{1,0:T(2,128)S(1)} copy(s32[2,1]{0,1:T(1,128)} %bitcast.5) | data formatting | bytes 16 | tf_op jit(solution)/shard_map/reshape | solution.py:369
  2.3 1.8 %copy.15.trans_ref = f32[8,165,165]{2,1,0:T(8,128)S(1)} copy(f32[8,165,165]{2,0,1:T(8,128)} %param.20) | data formatting | bytes 1742400 | tf_op args[9]
  4.1 0.0 copy-done
  4.1 0.0 copy-done.6
  4.1 0.0 copy-done.5
  4.1 0.0 copy-done.4
  4.1 0.0 copy-done.7
  4.1 0.0 copy-done.3
  4.2 0.0 copy-done.2
  4.2 0.0 copy-done.1
  4.2 19.0 %shard_map.122 = (f32[3,256]{1,0:T(4,128)S(1)}, f32[3,256]{1,0:T(4,128)S(1)}) custom-call(f32[3,256]{1,0:T(4,128)S(1)} %copy-done.1, f32[3,256]{1,0:T(4,128)S(1)} %copy-done.2, f32[3,256]{1,0:T(4,128)S(1)} %copy-done.3, f32[1,256]{1,0:T(1,128)S(1)} %bitcast.3, s32[2,1]{1,0:T(2,128)S(1)} %copy.13.occ_ref, s32[2,189]{1,0:T(2,128)S(1)} %copy-done.4, ...), custom_call_target="tpu_custom_call" | custom-call | tf_op jit(solution)/shard_map/pallas_call | solution.py:347
  23.1 0.6 %copy.18 = f32[3,256]{1,0:T(4,128)} copy(f32[3,256]{1,0:T(4,128)S(1)} %get-tuple-element.4) | data formatting | bytes 6144
  23.7 0.6 %copy.19 = f32[3,256]{1,0:T(4,128)} copy(f32[3,256]{1,0:T(4,128)S(1)} %get-tuple-element.5) | data formatting | bytes 6144
Async XLA Ops:
  0.6 3.5 %copy-start = (bf16[768,64]{1,0:T(8,128)(2,1)S(1)}, bf16[768,64]{1,0:T(8,128)(2,1)}, u32[]{:S(2)}) copy-start(bf16[768,64]{1,0:T(8,128)(2,1)} %constant.2.clone.pick_ref) | copy-start | bytes 294916
  0.6 3.5 %copy-start.6 = (f32[2,189]{1,0:T(2,128)S(1)}, f32[2,189]{1,0:T(2,128)}, u32[]{:S(2)}) copy-start(f32[2,189]{1,0:T(2,128)} %fscl_ref.1) | copy-start | bytes 4540
  0.7 3.5 %copy-start.5 = (s32[2,189]{1,0:T(2,128)S(1)}, s32[2,189]{1,0:T(2,128)}, u32[]{:S(2)}) copy-start(s32[2,189]{1,0:T(2,128)} %fcls_ref.1) | copy-start | bytes 4540
  0.7 3.5 %copy-start.4 = (s32[2,189]{1,0:T(2,128)S(1)}, s32[2,189]{1,0:T(2,128)}, u32[]{:S(2)}) copy-start(s32[2,189]{1,0:T(2,128)} %fbox_ref.1) | copy-start | bytes 4540
  0.7 3.5 %copy-start.7 = (f32[256]{0:T(256)S(1)}, f32[256]{0:T(256)}, u32[]{:S(2)}) copy-start(f32[256]{0:T(256)} %param.14) | copy-start | bytes 3076
  0.7 3.5 %copy-start.3 = (f32[3,256]{1,0:T(4,128)S(1)}, f32[3,256]{1,0:T(4,128)}, u32[]{:S(2)}) copy-start(f32[3,256]{1,0:T(4,128)} %pos_ref.1) | copy-start | bytes 9220
  0.7 3.5 %copy-start.2 = (f32[3,256]{1,0:T(4,128)S(1)}, f32[3,256]{1,0:T(4,128)}, u32[]{:S(2)}) copy-start(f32[3,256]{1,0:T(4,128)} %perm_ref.1) | copy-start | bytes 9220
  0.7 3.5 %copy-start.1 = (f32[3,256]{1,0:T(4,128)S(1)}, f32[3,256]{1,0:T(4,128)}, u32[]{:S(2)}) copy-start(f32[3,256]{1,0:T(4,128)} %dip_ref.1) | copy-start | bytes 9220

commit v2 on v1

--- a/solution.py
+++ b/solution.py
@@ -109,7 +109,8 @@
     lane = lax.broadcasted_iota(jnp.int32, (1, 2 * TILE), 1)
     second = lane >= TILE
     slot = jnp.where(second, lane - TILE, lane)
-    live = (slot < jnp.where(second, occ_ref[1:2], occ_ref[0:1])).astype(F32)
+    occ = occ_ref[...]
+    live = (slot < jnp.where(second, occ[:, 1:2], occ[:, 0:1])).astype(F32)
     pol = pol_ref[...]
     root = lax.rsqrt(pol)
     pos = pos_ref[...]
@@ -183,12 +184,12 @@
             device_id_type=MESH,
         )
 
-    def build(number, load, shift):
+    def build(layers, size):
         def body(block, carry):
-            rows = pl.ds(pl.multiple_of(block * ROWS, ROWS), ROWS)
+            rows = pl.ds(pl.multiple_of(block * size, size), size)
             target = geo_t[rows, :]
             total = [None] * 3
-            for half in range(2):
+            for number, load, shift, half in [one + (h,) for one in layers for h in range(2)]:
                 geo = load(half)
                 delta = [target[:, axis : axis + 1] - geo[axis : axis + 1] for axis in range(2)]
                 delta.append(target[:, 2:3] - (geo[2:3] + 2.0 * HALF * shift))
@@ -203,8 +204,8 @@
                 direct = lambda_three * cube
                 radial = 3.0 * lambda_five * (cube * inverse_two)
                 if number == 0:
-                    shape = (ROWS, TILE)
-                    here = block * ROWS + lax.broadcasted_iota(jnp.int32, shape, 0)
+                    shape = (size, TILE)
+                    here = block * size + lax.broadcasted_iota(jnp.int32, shape, 0)
                     other = half * TILE + lax.broadcasted_iota(jnp.int32, shape, 1)
                     keep = here != other
                     direct = jnp.where(keep, direct, 0.0)
@@ -222,13 +223,13 @@
                     tensor[2 * number + half, index, rows, :] = entry
                 total = gather(total, entries, [geo[4:5], geo[5:6], geo[6:7]])
             for axis in range(3):
-                if number == 0:
+                if layers[0][0] == 0:
                     acc[axis, rows, :] = total[axis]
                 else:
                     acc[axis, rows, :] += total[axis]
             return carry
 
-        lax.fori_loop(0, 2 * TILE // ROWS, body, 0)
+        lax.fori_loop(0, 2 * TILE // size, body, 0)
 
     def gather(total, m, q):
         terms = [
@@ -267,7 +268,7 @@
             total = part if total is None else total + part
         return total[0:3]
 
-    build(0, lambda half: own[0, :, half * TILE : (half + 1) * TILE], 0.0)
+    build([(0, lambda half: own[0, :, half * TILE : (half + 1) * TILE], 0.0)], 32)
 
     ilist = fbox_ref.shape[1]
     flat_rows = window.shape[0] * 8
@@ -286,7 +287,7 @@
         match = (fbox_ref[box : box + 1] == number).astype(F32).astype(BF16)
         inside = line & 7
         mine = jnp.logical_and(inside >= 3 * box, inside < 3 * box + 3)
-        mine = jnp.logical_and(mine, entry < fcnt_ref[box : box + 1])
+        mine = jnp.logical_and(mine, entry < fcnt_ref[...][:, box : box + 1])
         mine = jnp.logical_and(mine, fcls_ref[box : box + 1] == (line >> 3))
         weights = split(jnp.where(mine, fscl_ref[box : box + 1], 0.0))
         part = dot(weights[0], match, LANES) + dot(weights[1], match, LANES)
@@ -298,23 +299,30 @@
     selector = split(jnp.where(left == right, selector, 0.0))
 
     near_wait(0)
-    for side, shift in enumerate((-1.0, 1.0)):
-        build(
-            side + 1,
-            lambda half, side=side: beside[0, side, :, half * TILE : (half + 1) * TILE],
-            shift,
-        )
+    build(
+        [
+            (side + 1, lambda half, side=side: beside[0, side, :, half * TILE : (half + 1) * TILE], shift)
+            for side, shift in enumerate((-1.0, 1.0))
+        ],
+        16,
+    )
     near_zero = collect()
 
+    nterm, classes = trans_ref.shape[:2]
+    shifted = split(trans_ref[...].reshape(nterm * classes, nterm))
+    fold_shape = (nterm * classes, nterm)
+    fold = lax.broadcasted_iota(jnp.int32, fold_shape, 0) >> 3
+    fold = (fold == lax.broadcasted_iota(jnp.int32, fold_shape, 1)).astype(F32).astype(BF16)
     far_peers(lambda peer_group, step: far_copy(peer_group, step).wait_recv())
     summed = dot_parts(selector, split(window[...].reshape(flat_rows, WIDE)), PLAIN)
-    nterm = trans_ref.shape[1]
-    local = None
-    for index in range(trans_ref.shape[0]):
-        part = dot_parts(
-            split(summed[8 * index : 8 * index + 8, 0:nterm]), split(trans_ref[index]), LANES
-        )
-        local = part if local is None else local + part
+    moved = dot_parts(split(summed[:, 0:nterm]), shifted, LANES)
+    wanted = lax.broadcasted_iota(jnp.int32, (8, nterm * classes), 1) & 7
+    merged = None
+    for index in range(classes):
+        part = jnp.where(wanted == index, moved[8 * index : 8 * index + 8], 0.0)
+        merged = part if merged is None else merged + part
+    merged = split(merged)
+    local = dot(merged[0], fold, PLAIN) + dot(merged[1], fold, PLAIN)
     spread = dot_parts(split(local), split(mono_ref[0:nterm]), PLAIN)
     far_part = jnp.where(second, spread[3:6], spread[0:3])
 
@@ -366,8 +374,8 @@
                 collective_id=0, has_side_effects=True, vmem_limit_bytes=40 * 1024 * 1024
             ),
         )(
-            dip, perm, pos, pol.reshape(1, -1), occ.reshape(-1, 1), fbox, fcls, fcnt.reshape(-1, 1),
-            fscl, trans,
+            dip, perm, pos, pol.reshape(1, -1), occ.reshape(1, -1), fbox, fcls, fcnt.reshape(1, -1),
+            fscl, jnp.transpose(trans, (1, 0, 2)),
             jnp.asarray(pick_matrix(), BF16),
         )
 

time: 24.5 us -> 28.1 us (1.15)
  local copies, waits for them, and re-layouts: 4.6 us -> 9.53 us
  Pallas kernels: 19 us -> 17.5 us
    unnamed x19 -> x24, local copies, waits for them, and re-layouts: 2.99 us -> 9.53 us
    reshape x2 -> x0, local copies, waits for them, and re-layouts: 1.61 us -> none  [the longest x1 0.87 us: on_device(): occ.reshape(-1, 1)]
    pallas_call x1, Pallas kernels: 19 us -> 17.5 us  [on_device(): pl.pallas_call(functools.partial(kernel, groups, owners), out_shape=(jax....]
where the time goes in v2:
time: 28.1 us; the launch traced here: 27.7 us
  Pallas kernels  17.5 us (62%)
  local copies, waits for them, and re-layouts  9.53 us (34%)
  between operations  0.66 us (2%)
    pallas_call x1, Pallas kernels, on_device(): pl.pallas_call(functools.partial(kernel, groups, owners), out_shape=(jax....  17.5 us
    unnamed x24, local copies, waits for them, and re-layouts  9.53 us

profile of v2, /device:TPU:11, one launch (start us, length us, event | category | flops | bytes accessed | tf_op | source)
XLA Modules:
  0.0 27.7 jit_solution(7943258186157876558)
XLA Ops:
  0.6 0.0 copy-start
  0.6 1.3 %copy-done = f32[8,165,165]{2,0,1:T(8,128)S(1)} copy-done((f32[8,165,165]{2,0,1:T(8,128)S(1)}, f32[8,165,165]{2,0,1:T(8,128)}, u32[]{:S(2)}) %copy-start) | copy-done | bytes 871224
  2.0 0.0 copy-start.1
  2.0 0.9 %copy-done.1 = bf16[768,64]{1,0:T(8,128)(2,1)S(1)} copy-done((bf16[768,64]{1,0:T(8,128)(2,1)S(1)}, bf16[768,64]{1,0:T(8,128)(2,1)}, u32[]{:S(2)}) %copy-start.1) | copy-done | bytes 98328
  2.9 0.7 %copy-done.2 = f32[3,256]{1,0:T(4,128)S(1)} copy-done((f32[3,256]{1,0:T(4,128)S(1)}, f32[3,256]{1,0:T(4,128)}, u32[]{:S(2)}) %copy-start.2) | copy-done | bytes 3096
  3.6 0.0 copy-start.3
  3.6 0.7 %copy-done.3 = f32[3,256]{1,0:T(4,128)S(1)} copy-done((f32[3,256]{1,0:T(4,128)S(1)}, f32[3,256]{1,0:T(4,128)}, u32[]{:S(2)}) %copy-start.3) | copy-done | bytes 3096
  4.3 0.0 copy-start.4
  4.3 0.7 %copy-done.4 = f32[3,256]{1,0:T(4,128)S(1)} copy-done((f32[3,256]{1,0:T(4,128)S(1)}, f32[3,256]{1,0:T(4,128)}, u32[]{:S(2)}) %copy-start.4) | copy-done | bytes 3096
  5.0 0.0 copy-start.5
  5.0 0.7 %copy-done.5 = s32[2,189]{1,0:T(2,128)S(1)} copy-done((s32[2,189]{1,0:T(2,128)S(1)}, s32[2,189]{1,0:T(2,128)}, u32[]{:S(2)}) %copy-start.5) | copy-done | bytes 1536
  5.6 0.0 copy-start.6
  5.6 0.7 %copy-done.6 = s32[2,189]{1,0:T(2,128)S(1)} copy-done((s32[2,189]{1,0:T(2,128)S(1)}, s32[2,189]{1,0:T(2,128)}, u32[]{:S(2)}) %copy-start.6) | copy-done | bytes 1536
  6.3 0.0 copy-start.7
  6.3 0.7 %copy-done.7 = f32[2,189]{1,0:T(2,128)S(1)} copy-done((f32[2,189]{1,0:T(2,128)S(1)}, f32[2,189]{1,0:T(2,128)}, u32[]{:S(2)}) %copy-start.7) | copy-done | bytes 1536
  7.0 0.0 copy-start.8
  7.0 0.7 %copy-done.8 = f32[256]{0:T(256)S(1)} copy-done((f32[256]{0:T(256)S(1)}, f32[256]{0:T(256)}, u32[]{:S(2)}) %copy-start.8) | copy-done | bytes 1048
  7.7 0.0 copy-start.9
  7.7 0.7 %copy-done.9 = s32[2]{0:T(128)S(1)} copy-done((s32[2]{0:T(128)S(1)}, s32[2]{0:T(128)}, u32[]{:S(2)}) %copy-start.9) | copy-done | bytes 32
  8.3 0.0 copy-start.10
  8.3 0.7 %copy-done.10 = s32[2]{0:T(128)S(1)} copy-done((s32[2]{0:T(128)S(1)}, s32[2]{0:T(128)}, u32[]{:S(2)}) %copy-start.10) | copy-done | bytes 32
  9.0 17.5 %shard_map.122 = (f32[3,256]{1,0:T(4,128)S(1)}, f32[3,256]{1,0:T(4,128)S(1)}) custom-call(f32[3,256]{1,0:T(4,128)S(1)} %copy-done.2, f32[3,256]{1,0:T(4,128)S(1)} %copy-done.3, f32[3,256]{1,0:T(4,128)S(1)} %copy-done.4, f32[1,256]{1,0:T(1,128)S(1)} %bitcast.5, s32[1,2]{1,0:T(1,128)S(1)} %bitcast.6, s32[2,189]{1,0:T(2,128)S(1)} %copy-done.5, ...), custom_call_target="tpu_custom_call" | custom-call | tf_op jit(solution)/shard_map/pallas_call | solution.py:355
  26.5 0.6 %copy.15 = f32[3,256]{1,0:T(4,128)} copy(f32[3,256]{1,0:T(4,128)S(1)} %get-tuple-element.4) | data formatting | bytes 6144
  27.1 0.6 %copy.16 = f32[3,256]{1,0:T(4,128)} copy(f32[3,256]{1,0:T(4,128)S(1)} %get-tuple-element.5) | data formatting | bytes 6144
  (1 shorter events, 0.0 us)
Async XLA Ops:
  0.6 1.3 %copy-start = (f32[8,165,165]{2,0,1:T(8,128)S(1)}, f32[8,165,165]{2,0,1:T(8,128)}, u32[]{:S(2)}) copy-start(f32[8,165,165]{2,0,1:T(8,128)} %param.20) | copy-start | bytes 2613604
  2.0 0.9 %copy-start.1 = (bf16[768,64]{1,0:T(8,128)(2,1)S(1)}, bf16[768,64]{1,0:T(8,128)(2,1)}, u32[]{:S(2)}) copy-start(bf16[768,64]{1,0:T(8,128)(2,1)} %constant.2.clone.pick_ref) | copy-start | bytes 294916
  2.9 0.7 %copy-start.2 = (f32[3,256]{1,0:T(4,128)S(1)}, f32[3,256]{1,0:T(4,128)}, u32[]{:S(2)}) copy-start(f32[3,256]{1,0:T(4,128)} %dip_ref.1) | copy-start | bytes 9220
  3.6 0.7 %copy-start.3 = (f32[3,256]{1,0:T(4,128)S(1)}, f32[3,256]{1,0:T(4,128)}, u32[]{:S(2)}) copy-start(f32[3,256]{1,0:T(4,128)} %perm_ref.1) | copy-start | bytes 9220
  4.3 0.7 %copy-start.4 = (f32[3,256]{1,0:T(4,128)S(1)}, f32[3,256]{1,0:T(4,128)}, u32[]{:S(2)}) copy-start(f32[3,256]{1,0:T(4,128)} %pos_ref.1) | copy-start | bytes 9220
  5.0 0.7 %copy-start.5 = (s32[2,189]{1,0:T(2,128)S(1)}, s32[2,189]{1,0:T(2,128)}, u32[]{:S(2)}) copy-start(s32[2,189]{1,0:T(2,128)} %fbox_ref.1) | copy-start | bytes 4540
  5.6 0.7 %copy-start.6 = (s32[2,189]{1,0:T(2,128)S(1)}, s32[2,189]{1,0:T(2,128)}, u32[]{:S(2)}) copy-start(s32[2,189]{1,0:T(2,128)} %fcls_ref.1) | copy-start | bytes 4540
  6.3 0.7 %copy-start.7 = (f32[2,189]{1,0:T(2,128)S(1)}, f32[2,189]{1,0:T(2,128)}, u32[]{:S(2)}) copy-start(f32[2,189]{1,0:T(2,128)} %fscl_ref.1) | copy-start | bytes 4540
  7.0 0.7 %copy-start.8 = (f32[256]{0:T(256)S(1)}, f32[256]{0:T(256)}, u32[]{:S(2)}) copy-start(f32[256]{0:T(256)} %param.14) | copy-start | bytes 3076
  7.7 0.7 %copy-start.9 = (s32[2]{0:T(128)S(1)}, s32[2]{0:T(128)}, u32[]{:S(2)}) copy-start(s32[2]{0:T(128)} %param.15) | copy-start | bytes 28
  8.3 0.7 %copy-start.10 = (s32[2]{0:T(128)S(1)}, s32[2]{0:T(128)}, u32[]{:S(2)}) copy-start(s32[2]{0:T(128)} %param.18) | copy-start | bytes 28

commit v3 on v2

--- a/solution.py
+++ b/solution.py
@@ -64,7 +64,7 @@
     trans_ref, pick_ref,
     new_ref, res_ref,
     own, beside, geo_t, mono_ref, window, tensor, acc,
-    nsend, nrecv, wsend, wrecv,
+    nsend, nrecv, wsend, wrecv, fetches,
 ):
     group = lax.axis_index("group")
     layer = lax.axis_index("box")
@@ -106,6 +106,8 @@
             for turn in range(3):
                 beside[turn, side] = jnp.zeros((8, WIDE), F32)
 
+    for fetch in fetches[:-2] + fetches[-1:]:
+        fetch.wait()
     lane = lax.broadcasted_iota(jnp.int32, (1, 2 * TILE), 1)
     second = lane >= TILE
     slot = jnp.where(second, lane - TILE, lane)
@@ -308,6 +310,7 @@
     )
     near_zero = collect()
 
+    fetches[-2].wait()
     nterm, classes = trans_ref.shape[:2]
     shifted = split(trans_ref[...].reshape(nterm * classes, nterm))
     fold_shape = (nterm * classes, nterm)
@@ -346,18 +349,34 @@
     far_peers(lambda peer_group, step: far_copy(peer_group, step).wait_send())
 
 
+def staged(groups, owners, *refs):
+    given, results, held, rest, arrived = refs[:11], refs[11:13], refs[13:24], refs[24:-1], refs[-1]
+    fetches = [
+        pltpu.make_async_copy(given[index], held[index], arrived.at[index]) for index in range(11)
+    ]
+    for fetch in fetches:
+        fetch.start()
+    kernel(groups, owners, *held, *results, *rest, fetches)
+
+
 def solution(mesh):
     groups, owners = mesh.shape["group"], mesh.shape["box"]
 
     def on_device(dip, perm, pos, pol, occ, fbox, fcls, fcnt, fscl, trans):
         vmem = pl.BlockSpec(memory_space=pltpu.VMEM)
         slots = groups * SPAN
+        operands = (
+            dip, perm, pos, pol.reshape(1, -1), occ.reshape(1, -1), fbox, fcls,
+            fcnt.reshape(1, -1), fscl, jnp.transpose(trans, (1, 0, 2)),
+            jnp.asarray(pick_matrix(), BF16),
+        )
         return pl.pallas_call(
-            functools.partial(kernel, groups, owners),
+            functools.partial(staged, groups, owners),
             out_shape=(jax.ShapeDtypeStruct(dip.shape, F32),) * 2,
-            in_specs=[vmem] * 11,
+            in_specs=[pl.BlockSpec(memory_space=pltpu.HBM)] * 11,
             out_specs=(vmem, vmem),
-            scratch_shapes=[
+            scratch_shapes=[pltpu.VMEM(one.shape, one.dtype) for one in operands]
+            + [
                 pltpu.VMEM((3, 8, WIDE), F32),
                 pltpu.VMEM((3, 2, 8, WIDE), F32),
                 pltpu.VMEM((WIDE, 8), F32),
@@ -369,15 +388,12 @@
                 pltpu.SemaphoreType.DMA((6,)),
                 pltpu.SemaphoreType.DMA((slots,)),
                 pltpu.SemaphoreType.DMA((slots,)),
+                pltpu.SemaphoreType.DMA((11,)),
             ],
             compiler_params=pltpu.CompilerParams(
-                collective_id=0, has_side_effects=True, vmem_limit_bytes=40 * 1024 * 1024
+                collective_id=0, has_side_effects=True, vmem_limit_bytes=64 * 1024 * 1024
             ),
-        )(
-            dip, perm, pos, pol.reshape(1, -1), occ.reshape(1, -1), fbox, fcls, fcnt.reshape(1, -1),
-            fscl, jnp.transpose(trans, (1, 0, 2)),
-            jnp.asarray(pick_matrix(), BF16),
-        )
+        )(*operands)
 
     split_dim = ("group", "box")
     return jax.shard_map(

time: 28.1 us -> 21.5 us (0.77)
  local copies, waits for them, and re-layouts: 9.53 us -> 2.53 us
  Pallas kernels: 17.5 us -> 18 us
    unnamed x24 -> x2, local copies, waits for them, and re-layouts: 9.53 us -> 2.53 us
    pallas_call x1, Pallas kernels: 17.5 us -> 18 us  [on_device(): pl.pallas_call(functools.partial(staged, groups, owners), out_shape=(jax....]
where the time goes in v3:
time: 21.5 us; the launch traced here: 21.2 us
  Pallas kernels  18 us (84%)
  local copies, waits for them, and re-layouts  2.53 us (12%)
  between operations  0.64 us (3%)
    pallas_call x1, Pallas kernels, on_device(): pl.pallas_call(functools.partial(staged, groups, owners), out_shape=(jax....  18 us
    unnamed x2, local copies, waits for them, and re-layouts  2.53 us

profile of v3, /device:TPU:11, one launch (start us, length us, event | category | flops | bytes accessed | tf_op | source)
XLA Modules:
  0.0 21.2 jit_solution(2643060635393295434)
XLA Ops:
  0.6 18.0 %shard_map.122 = (f32[3,256]{1,0:T(4,128)}, f32[3,256]{1,0:T(4,128)}) custom-call(f32[3,256]{1,0:T(4,128)} %refs_0_.1, f32[3,256]{1,0:T(4,128)} %refs_1_.1, f32[3,256]{1,0:T(4,128)} %refs_2_.1, f32[1,256]{1,0:T(1,128)} %bitcast.5, s32[1,2]{1,0:T(1,128)} %bitcast.6, s32[2,189]{1,0:T(2,128)} %refs_5_.1, s32[2,189]{1,0:T(2,128)} %refs_6_.1, s32[1,2]{1,0:T(1,128)} %bitcast.7, ...), custom_call_target="tpu_custom_call" | custom-call | tf_op jit(solution)/shard_map/pallas_call | solution.py:373
  18.7 1.3 %copy.15 = f32[3,256]{1,0:T(4,128)} copy(f32[3,256]{1,0:T(4,128)} %get-tuple-element.4) | data formatting | bytes 6144
  20.0 1.3 %copy.16 = f32[3,256]{1,0:T(4,128)} copy(f32[3,256]{1,0:T(4,128)} %get-tuple-element.5) | data formatting | bytes 6144
